TPU v7x, 1024 devices: a whole 4x4x32 slice. The times are simulated.
1024 devices in a mesh: pair: 128 (over y, z), red: 8 (over x, core).
Axes of the slice: x: 4, y: 4, z: 32, core: 2. Of those that a mesh axis runs over, the one named last changes fastest.
Arguments:
- amplitudes: bfloat16 [1024, 8, 16, 64, 128], P('pair', 'red'), may hold values from -6 to 6
- integrals: bfloat16 [128, 8, 128, 128], P('pair', 'red'), may hold values from -0.09375 to 0.09375
- amp_mask: int32 [1024, 8, 16], P('pair', 'red'), may hold values 0 or 1
- kept_slab_indicator: int32 [128, 8], P('pair', 'red'), may hold values 0 or 1
Outputs:
- residual: bfloat16 [1024, 64, 1024], P('pair', 'red')
All inputs are finite; a program needn't handle non-finite values. No bound on the sum of `amp_mask` or of `kept_slab_indicator` on one device may be relied on, other than what follows from the above.
Results may differ from a plain program's by a relative error of at most 0.017.
Values may be sent and summed in bfloat16 or wider, within the bound.
A program may use at most 32 MiB of HBM per device.

v0:
```python
import jax
import jax.numpy as jnp
from jax import lax
from jax.sharding import PartitionSpec as P

NB = 8


def local(amplitudes, integrals, amp_mask, kept_slab_indicator):
    masked_amplitudes = amplitudes[:, 0] * amp_mask[:, 0, :, None, None].astype(jnp.bfloat16)
    slab_kept_markers = kept_slab_indicator.astype(jnp.bfloat16)
    virtual_pair_slabs = masked_amplitudes.shape[1]
    width = integrals.shape[3]
    all_tiles, every_block_kept = (
        lax.all_gather(integrals, "pair", axis=0, tiled=True),
        lax.all_gather(slab_kept_markers, "pair", axis=0, tiled=True),
    )
    scaled_contribution = all_tiles[:, 0] * every_block_kept[:, 0][:, None, None]
    grouped_blocks = scaled_contribution.reshape(NB, virtual_pair_slabs, width, width)
    product = jnp.einsum(
        "pkov,bkvw->pobw", masked_amplitudes, grouped_blocks, preferred_element_type=jnp.float32
    )
    partial_value = product.reshape(
        masked_amplitudes.shape[0], masked_amplitudes.shape[2], NB * width
    )
    summed = lax.psum_scatter(
        partial_value.astype(jnp.bfloat16), "red", scatter_dimension=1, tiled=True
    )
    return summed


def solution(mesh):
    return jax.shard_map(
        local,
        mesh=mesh,
        in_specs=(
            P("pair", "red", None, None, None),
            P("pair", "red", None, None),
            P("pair", "red", None),
            P("pair", "red"),
        ),
        out_specs=P("pair", "red", None),
        check_vma=False,
    )
```

profile of v0, /device:TPU:1, one launch (start us, length us, event | category | flops | bytes accessed | tf_op | source)
XLA Modules:
  0.0 359.7 jit_solution(15367625208132043644)
XLA Ops:
  6.5 0.0 all-gather.2.cloned.1.call-start
  6.5 0.7 all-gather.2.cloned.1.call-update
  7.3 0.0 reduce-scatter.4.cloned.1.call-start
  8.0 1.4 dynamic-slice
  9.3 0.8 dynamic-update-slice
  10.1 240.3 %all-reduce = bf16[128]{0:T(256)(128)(2,1)S(1)} all-reduce(bf16[128]{0:T(256)(128)(2,1)S(1)} %dynamic-update-slice), channel_id=1, replica_groups=mesh['pair'=128,'red'=8] {'pair'}, use_global_device_ids=true, to_apply=%add | all-reduce | flops 128 | bytes 512
  250.4 0.1 mul.25
  250.5 0.7 convert_bitcast_fusion
  251.2 24.2 %all-gather.2.cloned.1.call-done = bf16[128,1,128,128]{3,2,1,0:T(8,128)(2,1)} async-done(((bf16[1,1,128,128]{3,2,1,0:T(8,128)(2,1)}), bf16[128,1,128,128]{3,2,1,0:T(8,128)(2,1)}) %all-gather.2.cloned.1.call-update) | async-done | bytes 4194320 | tf_op jit(solution)/shard_map/all_gather | solution.py:15
  275.4 4.5 %fusion = bf16[8,128,16,128]{1,3,2,0:T(8,128)(2,1)} fusion(bf16[8,16]{1,0:T(8,128)(2,1)S(1)} %mul.25, bf16[8,16,128,128]{3,2,1,0:T(8,128)(2,1)} %bitcast.40), kind=kLoop, calls=%fused_computation.1 | loop fusion | flops 2097152 | bytes 8388864 | tf_op jit(solution)/shard_map/pkov,bkvw->pobw/dot_general | solution.py:20
  279.8 0.0 copy-start
  279.8 6.5 %copy.8 = bf16[8,128,16,128]{3,1,0,2:T(8,128)(2,1)} copy(bf16[8,128,16,128]{1,3,2,0:T(8,128)(2,1)} %fusion) | data formatting | bytes 8388608 | tf_op jit(solution)/shard_map/pkov,bkvw->pobw/dot_general | solution.py:20
  286.4 0.0 copy-done
  286.4 4.6 %fusion.7 = bf16[8,8,8,1024]{3,1,0,2:T(8,128)(2,1)S(1)} fusion(bf16[1024,16,128,1]{2,0,1,3:T(8,128)(2,1)} %bitcast.41, bf16[8,1,16,64,128]{4,3,2,1,0:T(8,128)(2,1)S(1)} %copy-done, bf16[8,16]{1,0:T(8,128)(2,1)S(1)} %convert_bitcast_fusion), kind=kOutput, calls=%fused_computation.9 | convolution fusion | flops 2149056512 | bytes 7340288 | tf_op jit(solution)/shard_map/pkov,bkvw->pobw/dot_general | solution.py:20
  290.9 1.1 copy.12
  292.0 0.0 reduce-scatter.4.cloned.1.call-update
  292.0 59.1 %reduce-scatter.4.cloned.1.call-done = bf16[8,8192]{1,0:T(8,128)(2,1)} async-done(((bf16[64,8192]{1,0:T(8,128)(2,1)}), bf16[8,8192]{1,0:T(8,128)(2,1)}) %reduce-scatter.4.cloned.1.call-update) | async-done | bytes 131088
  351.1 1.0 copy.16
  352.1 0.7 copy.11
  (1 shorter events, 0.0 us)
Async XLA Ops:
  6.5 268.8 %all-gather.2.cloned.1.call-start = ((), (), s32[]{:S(2)}) async-start(), calls=%async_computation.1 | async-start | bytes 4227072 | tf_op jit(solution)/shard_map/all_gather | solution.py:15
  7.3 343.9 %reduce-scatter.4.cloned.1.call-start = ((), (), s32[]{:S(2)}) async-start(), calls=%async_computation.2 | async-start | bytes 1179648
  279.8 6.6 %copy-start = (bf16[8,1,16,64,128]{4,3,2,1,0:T(8,128)(2,1)S(1)}, bf16[8,1,16,64,128]{4,3,2,1,0:T(8,128)(2,1)}, u32[]{:S(2)}) copy-start(bf16[8,1,16,64,128]{4,3,2,1,0:T(8,128)(2,1)} %param.4) | copy-start | bytes 6291460
Sparse Core Ops, SparseCore 0:
  11.5 263.8 all-gather.1
  292.2 58.8 reduce-scatter.3
where the time goes:
time: 360 us
  blocking collectives  240 us (67%)
  waiting for transfers between devices  83.9 us (23%)
  between operations  14.1 us (4%)
  local copies, waits for them, and re-layouts  11.6 us (3%)
  other arithmetic  5.18 us (1%)
  matrix products  4.55 us (1%)
    unnamed x1, blocking collectives  240 us
    unnamed x3, waiting for transfers between devices  59.8 us
    all_gather x1, waiting for transfers between devices, local(): lax.all_gather(integrals, 'pair', axis=0, tiled=True)  24.2 us
  transfers between devices with their start and end apart: 2, of which 2 were waited for; matrix products, arithmetic and copies ran while one was open for 1% of the time, Pallas kernels for 0%

commit v1 on v0

v1 whole, which is shorter than its diff:
```python
import functools

import jax
import jax.numpy as jnp
from jax import lax
from jax.experimental import pallas as pl
from jax.experimental.pallas import tpu as pltpu
from jax.sharding import PartitionSpec as P

MESH = pl.DeviceIdType.MESH
NY, NZ = 4, 32
PARTS = 2
EDGES = (
    (31, 0), (64, 0), (95, 31), (30, 31), (1, 0), (24, 0), (93, 95), (28, 30), (72, 64), (20, 24), (5, 1), (124, 28),
    (91, 93), (22, 24), (40, 72), (74, 72), (2, 1), (6, 5), (123, 124), (90, 91), (21, 22), (16, 20), (18, 20),
    (27, 123), (41, 40), (3, 2), (7, 6), (69, 5), (106, 74), (76, 74), (116, 20), (118, 22), (120, 24), (58, 90),
    (53, 21), (50, 18), (59, 27), (10, 106), (14, 16), (26, 58), (99, 3), (39, 7), (42, 41), (78, 74), (112, 16),
    (114, 18), (84, 116), (86, 118), (15, 16), (17, 18), (19, 20), (23, 24), (96, 0), (34, 2), (68, 69), (102, 6),
    (104, 72), (73, 74), (44, 76), (77, 76), (85, 53), (121, 120), (92, 124), (94, 30), (4, 3), (8, 104), (9, 41),
    (11, 10), (12, 44), (13, 14), (25, 26), (29, 28), (32, 96), (33, 1), (97, 1), (65, 1), (98, 2), (66, 34), (35, 3),
    (67, 99), (36, 68), (100, 99), (37, 5), (101, 5), (38, 39), (70, 102), (103, 7), (71, 39), (105, 73), (43, 42),
    (107, 106), (75, 76), (108, 76), (45, 77), (109, 77), (46, 78), (110, 78), (47, 15), (111, 112), (79, 78),
    (48, 50), (80, 112), (49, 50), (113, 114), (81, 17), (82, 50), (51, 19), (115, 116), (83, 84), (52, 20),
    (117, 85), (54, 22), (55, 23), (119, 120), (87, 86), (56, 24), (88, 24), (57, 59), (89, 121), (122, 123),
    (60, 92), (61, 93), (125, 93), (62, 94), (126, 30), (63, 95), (127, 95),
)
ORDER = (
    (0, 31), (1, 1), (1, 31), (0, 1), (1, 32), (0, 96), (0, 64), (1, 64), (0, 30), (1, 2), (1, 127), (1, 30), (0, 2),
    (0, 97), (1, 63), (0, 95), (1, 65), (0, 33), (0, 24), (1, 8), (1, 27), (1, 95), (0, 5), (0, 65), (1, 96),
    (0, 126), (1, 34), (0, 32), (1, 29), (0, 34), (0, 3), (0, 28), (1, 4), (0, 94), (1, 62), (1, 126), (1, 66),
    (0, 127), (0, 98), (1, 97), (0, 63), (0, 93), (1, 33), (1, 67), (1, 40), (0, 120), (0, 56), (0, 23), (1, 9),
    (0, 22), (1, 104), (1, 10), (1, 59), (1, 26), (0, 6), (1, 123), (1, 91), (0, 37), (1, 88), (0, 72), (0, 101),
    (1, 28), (0, 88), (0, 4), (1, 61), (1, 3), (0, 69), (0, 29), (0, 99), (1, 36), (1, 72), (0, 124), (0, 66),
    (0, 20), (1, 12), (1, 125), (0, 35), (0, 62), (1, 98), (1, 39), (1, 94), (0, 125), (1, 41), (0, 61), (1, 69),
    (1, 99), (0, 119), (0, 121), (0, 91), (1, 35), (0, 55), (0, 21), (1, 11), (1, 105), (1, 42), (1, 25), (0, 7),
    (0, 118), (0, 54), (1, 92), (1, 106), (1, 58), (0, 102), (1, 120), (1, 60), (0, 40), (0, 104), (1, 86), (1, 37),
    (0, 68), (1, 56), (0, 74), (1, 93), (0, 100), (0, 123), (0, 67), (1, 68), (0, 92), (1, 44), (0, 116), (0, 52),
    (1, 13), (0, 19), (1, 108), (1, 71), (0, 89), (0, 53), (1, 107), (1, 70), (1, 74), (0, 90), (1, 121), (1, 14),
    (0, 18), (0, 39), (0, 103), (1, 57), (0, 86), (1, 124), (1, 119), (0, 70), (0, 41), (1, 90), (1, 54), (1, 87),
    (0, 106), (1, 5), (0, 8), (1, 16), (0, 36), (0, 16), (0, 27), (0, 73), (1, 24), (1, 84), (1, 38), (1, 100),
    (0, 60), (1, 76), (0, 122), (0, 84), (1, 45), (0, 51), (0, 115), (0, 76), (1, 109), (0, 85), (1, 75), (1, 102),
    (0, 58), (1, 15), (0, 50), (0, 17), (1, 110), (1, 46), (1, 73), (0, 114), (1, 122), (0, 71), (0, 38), (1, 89),
    (0, 87), (1, 23), (1, 118), (0, 9), (1, 82), (0, 42), (0, 10), (1, 53), (1, 22), (0, 107), (1, 48), (0, 78),
    (1, 55), (0, 59), (0, 15), (1, 101), (1, 17), (0, 105), (0, 112), (1, 85), (1, 116), (1, 83), (1, 52), (0, 14),
    (0, 108), (0, 83), (0, 44), (1, 77), (0, 117), (0, 75), (1, 18), (1, 43), (0, 77), (1, 6), (0, 26), (1, 78),
    (0, 49), (1, 111), (0, 82), (1, 47), (0, 113), (0, 48), (1, 50), (1, 117), (0, 43), (1, 81), (1, 112), (1, 79),
    (0, 46), (0, 11), (1, 114), (1, 21), (0, 81), (1, 49), (1, 80), (1, 113), (0, 79), (0, 110), (0, 80), (0, 111),
    (0, 47), (1, 51), (1, 20), (0, 12), (0, 13), (0, 57), (1, 19), (1, 115), (0, 45), (1, 103), (0, 25), (1, 7),
    (0, 109),
)


def split(code):
    return code // NZ, code % NZ


def mirrored(code):
    oy, oz = split(code)
    return (-oy % NY) * NZ + -oz % NZ


def plan():
    children = {}
    for child, parent in EDGES:
        for part in range(PARTS):
            turn = mirrored if part % 2 else (lambda code: code)
            children.setdefault((part, turn(parent)), []).append(turn(child))
    return children


def kernel(
    red, amp_ref, int_ref, mask_ref, kept_ref, out_ref,
    raw, lhs, tiles, total, part, landed,
    amp_sem, send_sem, recv_sem, red_send, red_recv,
):
    pair, me = lax.axis_index("pair"), lax.axis_index("red")
    y, z = lax.div(pair, NZ), lax.rem(pair, NZ)
    children = plan()
    step = tiles.shape[2] // PARTS
    pairs, slabs, occ, width = raw.shape
    group = 2 * width

    def at(oy, oz):
        return lax.rem(y + (oy % NY), NY), lax.rem(z + (oz % NZ), NZ)

    def chip(oy, oz):
        ny, nz = at(oy, oz)
        return (ny * NZ + nz, me)

    def copy(piece, child, parent):
        cy, cz = split(child)
        py, pz = split(parent)
        sy, sz = at(-py, -pz)
        slot = tiles.at[sy, sz, pl.ds(piece * step, step)]
        return pltpu.make_async_remote_copy(
            src_ref=slot, dst_ref=slot,
            send_sem=send_sem.at[piece * NY * NZ + child],
            recv_sem=recv_sem.at[piece * NY * NZ + child],
            device_id=chip(cy - py, cz - pz), device_id_type=MESH,
        )

    load = pltpu.make_async_copy(amp_ref.at[:, 0], raw, amp_sem)
    load.start()

    hops = set()
    for (piece, parent), below in children.items():
        for child in below:
            (cy, cz), (py, pz) = split(child), split(parent)
            hop = ((cy - py) % NY, (cz - pz) % NZ)
            hops |= {hop, (-hop[0] % NY, -hop[1] % NZ)}
    hops = sorted(hops)
    barrier = pltpu.get_barrier_semaphore()
    for hop in hops:
        pl.semaphore_signal(barrier, 1, device_id=chip(*hop), device_id_type=MESH)
    for d in range(1, red):
        pl.semaphore_signal(barrier, 1, device_id=(pair, lax.rem(me + d, red)), device_id_type=MESH)

    kept = kept_ref[0, 0].astype(jnp.float32)
    tiles[y, z] = (int_ref[0, 0].astype(jnp.float32) * kept).astype(jnp.bfloat16)
    pl.semaphore_wait(barrier, len(hops) + red - 1)

    def forward(piece, code):
        for child in children.get((piece, code), ()):
            copy(piece, child, code).start()

    for piece in range(PARTS):
        forward(piece, 0)

    load.wait()

    @pl.loop(0, pairs)
    def _(p):
        rows = pl.ds(pl.multiple_of(p * occ, occ), occ)
        for k in range(slabs):
            weight = mask_ref[p, 0, k].astype(jnp.float32).astype(jnp.bfloat16)
            lhs[rows, k * width:(k + 1) * width] = raw[p, k] * weight

    def red_copy(g, d):
        owner = lax.rem(me + d, red)
        return pltpu.make_async_remote_copy(
            src_ref=part.at[g, owner], dst_ref=landed.at[g, me],
            send_sem=red_send.at[g, d], recv_sem=red_recv.at[g, d],
            device_id=(pair, owner), device_id_type=MESH,
        )

    def multiply(g):
        column, _ = at(-g, 0)
        rhs = jnp.concatenate(
            [tiles[column, h * slabs:(h + 1) * slabs].reshape(slabs * width, width) for h in range(2)], axis=1
        )
        total[...] = jnp.dot(lhs[...], rhs, preferred_element_type=jnp.float32)
        low = occ // red
        for j in range(red):
            rows = [total[p * occ + j * low:p * occ + (j + 1) * low, :] for p in range(pairs)]
            part[g, j] = jnp.concatenate(rows, axis=0).astype(jnp.bfloat16)
        for d in range(1, red):
            red_copy(g, d).start()

    def finish(g):
        column, _ = at(-g, 0)
        value = part[g, me].astype(jnp.float32)
        for d in range(1, red):
            red_copy(g, d).wait_recv()
            value = value + landed[g, lax.rem(me + red - d, red)].astype(jnp.float32)
        spot = pl.ds(pl.multiple_of(column * group, group), group)
        out_ref[:, :, spot] = value.reshape(pairs, occ // red, group).astype(jnp.bfloat16)

    missing = {g: PARTS * NZ for g in range(NY)}
    missing[0] -= PARTS
    done = []
    for piece, code in ORDER:
        copy(piece, code, code).wait_recv()
        forward(piece, code)
        g = code // NZ
        missing[g] -= 1
        if missing[g] == 0:
            multiply(g)
            done.append(g)
            if len(done) > 1:
                finish(done[-2])
    finish(done[-1])

    for (piece, parent), below in children.items():
        for child in below:
            copy(piece, child, parent).wait_send()
    for g in range(NY):
        for d in range(1, red):
            red_copy(g, d).wait_send()


def local(red, amplitudes, integrals, amp_mask, kept_slab_indicator):
    pairs, _, slabs, occ, width = amplitudes.shape
    rows, group = pairs * occ, 2 * width
    out = jax.ShapeDtypeStruct((pairs, occ // red, NY * group), jnp.bfloat16)
    dma = pltpu.SemaphoreType.DMA
    return pl.pallas_call(
        functools.partial(kernel, red),
        out_shape=out,
        in_specs=[
            pl.BlockSpec(memory_space=pl.ANY),
            pl.BlockSpec(memory_space=pltpu.VMEM),
            pl.BlockSpec(memory_space=pltpu.SMEM),
            pl.BlockSpec(memory_space=pltpu.SMEM),
        ],
        out_specs=pl.BlockSpec(memory_space=pltpu.VMEM),
        scratch_shapes=[
            pltpu.VMEM((pairs, slabs, occ, width), jnp.bfloat16),
            pltpu.VMEM((rows, slabs * width), jnp.bfloat16),
            pltpu.VMEM((NY, NZ, width, width), jnp.bfloat16),
            pltpu.VMEM((rows, group), jnp.float32),
            pltpu.VMEM((NY, red, rows // red, group), jnp.bfloat16),
            pltpu.VMEM((NY, red, rows // red, group), jnp.bfloat16),
            dma, dma((PARTS * NY * NZ,)), dma((PARTS * NY * NZ,)), dma((NY, red)), dma((NY, red)),
        ],
        compiler_params=pltpu.CompilerParams(
            collective_id=0, has_side_effects=True, vmem_limit_bytes=48 * 1024 * 1024
        ),
    )(amplitudes, integrals, amp_mask, kept_slab_indicator)


def solution(mesh):
    return jax.shard_map(
        functools.partial(local, mesh.shape["red"]),
        mesh=mesh,
        in_specs=(
            P("pair", "red", None, None, None),
            P("pair", "red", None, None),
            P("pair", "red", None),
            P("pair", "red"),
        ),
        out_specs=P("pair", "red", None),
        check_vma=False,
    )
```

time: 360 us -> 85.6 us (0.24)
  blocking collectives: 240 us -> 0 us
  waiting for transfers between devices: 83.9 us -> 0 us
  Pallas kernels: 0 us -> 81 us
  between operations: 14.1 us -> 0.67 us
  local copies, waits for them, and re-layouts: 11.6 us -> 3.69 us
  other arithmetic: 5.18 us -> 0 us
  matrix products: 4.55 us -> 0 us
    unnamed x1 -> x0, blocking collectives: 240 us -> none
    pallas_call x0 -> x1, Pallas kernels: none -> 81 us  [local(): pl.pallas_call(functools.partial(kernel, red), out_shape=out, in_specs=[p...]
    unnamed x3 -> x0, waiting for transfers between devices: 59.8 us -> none
    all_gather x1 -> x0, waiting for transfers between devices: 24.2 us -> none  [local(): lax.all_gather(integrals, 'pair', axis=0, tiled=True)]
    dot_general x1 -> x0, local copies, waits for them, and re-layouts: 6.55 us -> none  [local(): jnp.einsum('pkov,bkvw->pobw', masked_amplitudes, grouped_blocks, preferre...]
    dot_general x1 -> x0, matrix products: 4.55 us -> none  [local(): jnp.einsum('pkov,bkvw->pobw', masked_amplitudes, grouped_blocks, preferre...]
    dot_general x1 -> x0, other arithmetic: 4.49 us -> none  [local(): jnp.einsum('pkov,bkvw->pobw', masked_amplitudes, grouped_blocks, preferre...]
  transfers between devices with their start and end apart: 2 -> 0, of which waited for: 2 -> 0; matrix products, arithmetic and copies ran while one was open for 1% -> 0% of each run, Pallas kernels for 0% -> 0%
where the time goes in v1:
time: 85.6 us; the launch traced here: 85.3 us
  Pallas kernels  81 us (95%)
  local copies, waits for them, and re-layouts  3.69 us (4%)
    pallas_call x1, Pallas kernels, local(): pl.pallas_call(functools.partial(kernel, red), out_shape=out, in_specs=[p...  81 us
    unnamed x7, local copies, waits for them, and re-layouts  3.69 us

profile of v1, /device:TPU:1, one launch (start us, length us, event | category | flops | bytes accessed | tf_op | source)
XLA Modules:
  0.0 85.3 jit_solution(4432203366680088429)
XLA Ops:
  0.7 0.0 copy-start
  0.7 1.6 %copy-done = bf16[8,1,16,64,128]{4,3,2,1,0:T(8,128)(2,1)S(1)} copy-done((bf16[8,1,16,64,128]{4,3,2,1,0:T(8,128)(2,1)S(1)}, bf16[8,1,16,64,128]{4,3,2,1,0:T(8,128)(2,1)}, u32[]{:S(2)}) %copy-start) | copy-done | bytes 2097176
  2.2 0.0 copy-start.1
  2.2 0.8 copy-done.1
  3.0 0.0 copy-start.2
  3.0 0.7 copy-done.2
  3.7 81.0 %shard_map.46 = bf16[8,8,1024]{2,1,0:T(8,128)(2,1)S(1)} custom-call(bf16[8,1,16,64,128]{4,3,2,1,0:T(8,128)(2,1)S(1)} %copy-done, bf16[1,1,128,128]{3,2,1,0:T(8,128)(2,1)S(1)} %copy-done.1, s32[8,1,16]{2,1,0:T(1,128)S(1)} %copy-done.2, s32[1,1]{1,0:T(1,128)S(6)} %copy.6.kept_ref), custom_call_target="tpu_custom_call" | custom-call | tf_op jit(solution)/shard_map/pallas_call | solution.py:196
  84.7 0.7 copy.7
Async XLA Ops:
  0.7 1.6 %copy-start = (bf16[8,1,16,64,128]{4,3,2,1,0:T(8,128)(2,1)S(1)}, bf16[8,1,16,64,128]{4,3,2,1,0:T(8,128)(2,1)}, u32[]{:S(2)}) copy-start(bf16[8,1,16,64,128]{4,3,2,1,0:T(8,128)(2,1)} %amp_ref.1) | copy-start | bytes 6291460
  2.2 0.8 copy-start.1
  3.0 0.7 copy-start.2

commit v2 on v1

v2 whole, which is shorter than its diff:
```python
import functools

import jax
import jax.numpy as jnp
from jax import lax
from jax.experimental import pallas as pl
from jax.experimental.pallas import tpu as pltpu
from jax.sharding import PartitionSpec as P

MESH = pl.DeviceIdType.MESH
NY, NZ = 4, 32
EDGES = (
    (25, 0), (1, 0), (31, 0), (9, 1), (29, 31), (3, 0), (24, 25), (61, 29), (18, 25), (23, 24), (5, 3), (10, 9),
    (60, 61), (12, 9), (21, 23), (6, 5), (33, 1), (41, 9), (55, 23), (59, 60), (106, 10), (127, 31), (15, 12),
    (13, 12), (114, 18), (4, 3), (7, 6), (17, 18), (19, 18), (20, 21), (27, 59), (34, 33), (54, 55), (57, 25),
    (73, 41), (74, 106), (93, 61), (101, 5), (119, 23), (121, 25), (126, 127), (14, 13), (82, 114), (108, 12),
    (2, 34), (11, 10), (16, 17), (36, 4), (38, 6), (40, 41), (45, 13), (47, 15), (49, 17), (51, 19), (56, 24),
    (58, 57), (72, 73), (75, 74), (86, 54), (92, 93), (94, 126), (102, 101), (103, 7), (113, 17), (116, 20),
    (118, 119), (122, 121), (123, 27), (64, 0), (65, 1), (67, 3), (78, 14), (80, 82), (95, 31), (110, 108), (8, 40),
    (22, 23), (26, 122), (28, 29), (30, 29), (32, 0), (35, 3), (37, 38), (39, 40), (42, 74), (43, 11), (44, 12),
    (46, 14), (48, 16), (50, 49), (52, 51), (53, 54), (62, 94), (63, 31), (66, 34), (68, 36), (69, 101), (70, 102),
    (71, 72), (76, 75), (77, 45), (79, 47), (81, 82), (83, 51), (84, 116), (85, 86), (87, 86), (88, 56), (89, 121),
    (90, 58), (91, 123), (96, 0), (97, 1), (98, 2), (99, 3), (100, 4), (104, 103), (105, 9), (107, 108), (109, 13),
    (111, 15), (112, 113), (115, 114), (117, 118), (120, 24), (124, 92), (125, 29),
)
ORDER = (
    (0, 1), (1, 31), (0, 96), (1, 32), (0, 31), (1, 1), (0, 32), (1, 96), (0, 64), (1, 64), (0, 3), (1, 29), (0, 33),
    (1, 127), (0, 97), (1, 63), (0, 127), (1, 33), (0, 29), (1, 3), (0, 63), (1, 97), (0, 25), (1, 7), (0, 65),
    (1, 95), (0, 95), (1, 65), (0, 99), (1, 61), (0, 4), (1, 28), (0, 35), (1, 125), (0, 67), (1, 93), (0, 34),
    (1, 126), (0, 5), (1, 27), (0, 126), (1, 34), (0, 61), (1, 99), (0, 30), (1, 2), (0, 125), (1, 35), (0, 28),
    (1, 4), (0, 24), (1, 8), (0, 121), (1, 39), (0, 57), (1, 103), (0, 9), (1, 23), (0, 36), (1, 124), (0, 100),
    (1, 60), (0, 2), (1, 30), (0, 6), (1, 26), (0, 66), (1, 94), (0, 101), (1, 59), (0, 60), (1, 100), (0, 94),
    (1, 66), (0, 93), (1, 67), (0, 23), (1, 9), (0, 56), (1, 104), (0, 122), (1, 38), (0, 120), (1, 40), (0, 58),
    (1, 102), (0, 89), (1, 71), (0, 10), (1, 22), (0, 41), (1, 119), (0, 105), (1, 55), (0, 18), (1, 14), (0, 68),
    (1, 92), (0, 98), (1, 62), (0, 7), (1, 25), (0, 38), (1, 122), (0, 102), (1, 58), (0, 69), (1, 91), (0, 12),
    (1, 20), (0, 59), (1, 101), (0, 62), (1, 98), (0, 92), (1, 68), (0, 55), (1, 105), (0, 119), (1, 41), (0, 22),
    (1, 10), (0, 88), (1, 72), (0, 26), (1, 6), (0, 11), (1, 21), (0, 21), (1, 11), (0, 90), (1, 70), (0, 40),
    (1, 120), (0, 106), (1, 54), (0, 17), (1, 15), (0, 73), (1, 87), (0, 19), (1, 13), (0, 114), (1, 46), (0, 37),
    (1, 123), (0, 103), (1, 57), (0, 70), (1, 90), (0, 13), (1, 19), (0, 108), (1, 52), (0, 44), (1, 116), (0, 54),
    (1, 106), (0, 27), (1, 5), (0, 124), (1, 36), (0, 118), (1, 42), (0, 43), (1, 117), (0, 20), (1, 12), (0, 15),
    (1, 17), (0, 8), (1, 24), (0, 39), (1, 121), (0, 74), (1, 86), (0, 16), (1, 16), (0, 113), (1, 47), (0, 72),
    (1, 88), (0, 49), (1, 111), (0, 115), (1, 45), (0, 51), (1, 109), (0, 104), (1, 56), (0, 82), (1, 78), (0, 14),
    (1, 18), (0, 45), (1, 115), (0, 109), (1, 51), (0, 107), (1, 53), (0, 86), (1, 74), (0, 123), (1, 37), (0, 53),
    (1, 107), (0, 110), (1, 50), (0, 116), (1, 44), (0, 117), (1, 43), (0, 47), (1, 113), (0, 75), (1, 85), (0, 111),
    (1, 49), (0, 112), (1, 48), (0, 42), (1, 118), (0, 71), (1, 89), (0, 48), (1, 112), (0, 50), (1, 110), (0, 83),
    (1, 77), (0, 52), (1, 108), (0, 46), (1, 114), (0, 81), (1, 79), (0, 77), (1, 83), (0, 87), (1, 73), (0, 80),
    (1, 80), (0, 91), (1, 69), (0, 78), (1, 82), (0, 85), (1, 75), (0, 84), (1, 76), (0, 79), (1, 81), (0, 76),
    (1, 84),
)
COLUMNS = (0, 1, 3, 2)


def split(code):
    return code // NZ, code % NZ


def mirrored(code):
    oy, oz = split(code)
    return (-oy % NY) * NZ + -oz % NZ


def plan():
    children = {}
    for child, parent in EDGES:
        children.setdefault((0, parent), []).append(child)
        children.setdefault((1, mirrored(parent)), []).append(mirrored(child))
    return children


def kernel(
    red, amp_ref, int_ref, mask_ref, kept_ref, out_ref,
    raw, lhs, own, mask, flag, tiles, total, part, met, pooled, landed,
    load_sem, send_sem, recv_sem, met_send, met_recv, red_send, red_recv,
):
    pair, me = lax.axis_index("pair"), lax.axis_index("red")
    y, z = lax.div(pair, NZ), lax.rem(pair, NZ)
    children = plan()
    inner = [node for node in ((0, 0), (1, 0)) + ORDER if node in children]
    sem_of = {node: NY + i for i, node in enumerate(inner)}
    pairs, slabs, occ, width = raw.shape
    group = 2 * width

    def at(oy, oz):
        return lax.rem(y + (oy % NY), NY), lax.rem(z + (oz % NZ), NZ)

    def chip(oy, oz):
        ny, nz = at(oy, oz)
        return (ny * NZ + nz, me)

    def copy(half, child, parent):
        cy, cz = split(child)
        py, pz = split(parent)
        sy, sz = at(-py, -pz)
        slot = tiles.at[(sy * NZ + sz) * 2 + half]
        return pltpu.make_async_remote_copy(
            src_ref=slot, dst_ref=slot,
            send_sem=send_sem, recv_sem=recv_sem.at[sem_of.get((half, child), child // NZ)],
            device_id=chip(cy - py, cz - pz), device_id_type=MESH,
        )

    def whole(count, sem):
        spot = tiles.at[pl.ds(0, count)]
        return pltpu.make_async_remote_copy(
            src_ref=spot, dst_ref=spot, send_sem=send_sem, recv_sem=recv_sem.at[sem],
            device_id=chip(0, 1), device_id_type=MESH,
        )

    loads = [
        pltpu.make_async_copy(src, dst, load_sem.at[i])
        for i, (src, dst) in enumerate(
            ((int_ref.at[0, 0], own), (kept_ref, flag), (mask_ref, mask), (amp_ref.at[:, 0], raw))
        )
    ]
    for load in loads:
        load.start()

    hops = set()
    for child, parent in EDGES:
        (cy, cz), (py, pz) = split(child), split(parent)
        hop = ((cy - py) % NY, (cz - pz) % NZ)
        hops |= {hop, (-hop[0] % NY, -hop[1] % NZ)}
    hops = sorted(hops)
    barrier = pltpu.get_barrier_semaphore()
    for hop in hops:
        pl.semaphore_signal(barrier, 1, device_id=chip(*hop), device_id_type=MESH)
    core, at_x, chips = lax.rem(me, 2), lax.div(me, 2), red // 2
    partners = [(pair, me + 1 - 2 * core)] + [(pair, lax.rem(at_x + d, chips) * 2 + core) for d in range(1, chips)]
    for partner in partners:
        pl.semaphore_signal(barrier, 1, device_id=partner, device_id_type=MESH)

    loads[0].wait()
    loads[1].wait()
    kept = flag[0, 0].astype(jnp.float32)
    mine = (own[...].astype(jnp.float32) * kept).astype(jnp.bfloat16)
    tiles[pl.ds(pair * 2, 2)] = mine.reshape(2, width // 2, width)
    pl.semaphore_wait(barrier, len(hops) + len(partners))

    def forward(half, code):
        for child in children.get((half, code), ()):
            copy(half, child, code).start()

    for half in range(2):
        forward(half, 0)

    loads[2].wait()
    loads[3].wait()

    @pl.loop(0, pairs)
    def _(p):
        rows = pl.ds(pl.multiple_of(p * occ, occ), occ)
        for k in range(slabs):
            weight = mask[p, 0, k].astype(jnp.float32).astype(jnp.bfloat16)
            lhs[rows, k * width:(k + 1) * width] = raw[p, k] * weight

    low = occ // red

    def met_copy(g):
        return pltpu.make_async_remote_copy(
            src_ref=part.at[g, 1 - core], dst_ref=met.at[g],
            send_sem=met_send.at[g], recv_sem=met_recv.at[g],
            device_id=(pair, me + 1 - 2 * core), device_id_type=MESH,
        )

    def red_copy(g, d):
        to = lax.rem(at_x + d, chips)
        return pltpu.make_async_remote_copy(
            src_ref=pooled.at[g, to], dst_ref=landed.at[g, at_x],
            send_sem=red_send.at[g, d], recv_sem=red_recv.at[g, d],
            device_id=(pair, to * 2 + core), device_id_type=MESH,
        )

    def multiply(g):
        column, _ = at(-g, 0)
        rhs = jnp.concatenate(
            [tiles[pl.ds((column * NZ + h * slabs) * 2, slabs * 2)].reshape(slabs * width, width) for h in range(2)], axis=1
        )
        total[...] = jnp.dot(lhs[...], rhs, preferred_element_type=jnp.float32)
        for j in range(red):
            rows = [total[p * occ + j * low:p * occ + (j + 1) * low, :] for p in range(pairs)]
            part[g, j % 2, j // 2] = jnp.concatenate(rows, axis=0).astype(jnp.bfloat16)
        met_copy(g).start()

    def pass_on(g):
        met_copy(g).wait_recv()
        pooled[g] = (part[g, core].astype(jnp.float32) + met[g].astype(jnp.float32)).astype(jnp.bfloat16)
        for d in range(1, chips):
            red_copy(g, d).start()

    def finish(g):
        column, _ = at(-g, 0)
        value = part[g, core, at_x].astype(jnp.float32) + met[g, at_x].astype(jnp.float32)
        for d in range(1, chips):
            red_copy(g, d).wait_recv()
            value = value + landed[g, lax.rem(at_x + chips - d, chips)].astype(jnp.float32)
        spot = pl.ds(pl.multiple_of(column * group, group), group)
        out_ref[:, :, spot] = value.reshape(pairs, low, group).astype(jnp.bfloat16)

    for half, code in inner:
        if code:
            copy(half, code, code).wait_recv()
            forward(half, code)
    before = None
    for g in COLUMNS:
        outer = sum(code // NZ == g and (half, code) not in sem_of for half, code in ORDER)
        if outer:
            whole(outer, g).wait_recv()
        multiply(g)
        if before is not None:
            pass_on(before)
        before = g
    finish(COLUMNS[0])
    pass_on(before)
    for g in COLUMNS[1:]:
        finish(g)

    whole(2 * len(EDGES), 0).wait_send()
    for g in range(NY):
        met_copy(g).wait_send()
        for d in range(1, chips):
            red_copy(g, d).wait_send()


def inner_count():
    return len({parent for _, parent in EDGES})


def local(red, amplitudes, integrals, amp_mask, kept_slab_indicator):
    pairs, _, slabs, occ, width = amplitudes.shape
    rows, group = pairs * occ, 2 * width
    out = jax.ShapeDtypeStruct((pairs, occ // red, NY * group), jnp.bfloat16)
    dma = pltpu.SemaphoreType.DMA
    return pl.pallas_call(
        functools.partial(kernel, red),
        out_shape=out,
        in_specs=[
            pl.BlockSpec(memory_space=pltpu.HBM),
            pl.BlockSpec(memory_space=pltpu.HBM),
            pl.BlockSpec(memory_space=pltpu.HBM),
            pl.BlockSpec(memory_space=pltpu.HBM),
        ],
        out_specs=pl.BlockSpec(memory_space=pltpu.VMEM),
        scratch_shapes=[
            pltpu.VMEM((pairs, slabs, occ, width), jnp.bfloat16),
            pltpu.VMEM((rows, slabs * width), jnp.bfloat16),
            pltpu.VMEM((width, width), jnp.bfloat16),
            pltpu.SMEM(amp_mask.shape, jnp.int32),
            pltpu.SMEM(kept_slab_indicator.shape, jnp.int32),
            pltpu.VMEM((NY * NZ * 2, width // 2, width), jnp.bfloat16),
            pltpu.VMEM((rows, group), jnp.float32),
            pltpu.VMEM((NY, 2, red // 2, rows // red, group), jnp.bfloat16),
            pltpu.VMEM((NY, red // 2, rows // red, group), jnp.bfloat16),
            pltpu.VMEM((NY, red // 2, rows // red, group), jnp.bfloat16),
            pltpu.VMEM((NY, red // 2, rows // red, group), jnp.bfloat16),
            dma((4,)), dma, dma((NY + 2 * inner_count(),)),
            dma((NY,)), dma((NY,)), dma((NY, red // 2)), dma((NY, red // 2)),
        ],
        compiler_params=pltpu.CompilerParams(
            collective_id=0, has_side_effects=True, vmem_limit_bytes=63 * 1024 * 1024
        ),
    )(amplitudes, integrals, amp_mask, kept_slab_indicator)


def solution(mesh):
    return jax.shard_map(
        functools.partial(local, mesh.shape["red"]),
        mesh=mesh,
        in_specs=(
            P("pair", "red", None, None, None),
            P("pair", "red", None, None),
            P("pair", "red", None),
            P("pair", "red"),
        ),
        out_specs=P("pair", "red", None),
        check_vma=False,
    )
```

time: 85.6 us -> 73.1 us (0.85)
  Pallas kernels: 81 us -> 70.7 us
  local copies, waits for them, and re-layouts: 3.69 us -> 1.57 us
    pallas_call x1, Pallas kernels: 81 us -> 70.7 us  [local(): pl.pallas_call(functools.partial(kernel, red), out_shape=out, in_specs=[p...]
    unnamed x7 -> x1, local copies, waits for them, and re-layouts: 3.69 us -> 1.57 us
where the time goes in v2:
time: 73.1 us; the launch traced here: 72.9 us
  Pallas kernels  70.7 us (97%)
  local copies, waits for them, and re-layouts  1.57 us (2%)
    pallas_call x1, Pallas kernels, local(): pl.pallas_call(functools.partial(kernel, red), out_shape=out, in_specs=[p...  70.7 us
    unnamed x1, local copies, waits for them, and re-layouts  1.57 us

profile of v2, /device:TPU:1, one launch (start us, length us, event | category | flops | bytes accessed | tf_op | source)
XLA Modules:
  0.0 72.9 jit_solution(11283201379701809707)
XLA Ops:
  0.7 70.7 %shard_map.46 = bf16[8,8,1024]{2,1,0:T(8,128)(2,1)} custom-call(bf16[8,1,16,64,128]{4,3,2,1,0:T(8,128)(2,1)} %amp_ref.1, bf16[1,1,128,128]{3,2,1,0:T(8,128)(2,1)} %int_ref.1, s32[8,1,16]{2,1,0:T(1,128)} %mask_ref.1, s32[1,1]{1,0:T(1,128)S(6)} %copy.6.kept_ref), custom_call_target="tpu_custom_call" | custom-call | tf_op jit(solution)/shard_map/pallas_call | solution.py:232
  71.3 1.6 %copy.7 = bf16[8,8,1024]{2,1,0:T(8,128)(2,1)} copy(bf16[8,8,1024]{2,1,0:T(8,128)(2,1)} %shard_map.46) | data formatting | bytes 262144

commit v3 on v2

--- a/solution.py
+++ b/solution.py
@@ -10,42 +10,41 @@
 MESH = pl.DeviceIdType.MESH
 NY, NZ = 4, 32
 EDGES = (
-    (25, 0), (1, 0), (31, 0), (9, 1), (29, 31), (3, 0), (24, 25), (61, 29), (18, 25), (23, 24), (5, 3), (10, 9),
-    (60, 61), (12, 9), (21, 23), (6, 5), (33, 1), (41, 9), (55, 23), (59, 60), (106, 10), (127, 31), (15, 12),
-    (13, 12), (114, 18), (4, 3), (7, 6), (17, 18), (19, 18), (20, 21), (27, 59), (34, 33), (54, 55), (57, 25),
-    (73, 41), (74, 106), (93, 61), (101, 5), (119, 23), (121, 25), (126, 127), (14, 13), (82, 114), (108, 12),
-    (2, 34), (11, 10), (16, 17), (36, 4), (38, 6), (40, 41), (45, 13), (47, 15), (49, 17), (51, 19), (56, 24),
-    (58, 57), (72, 73), (75, 74), (86, 54), (92, 93), (94, 126), (102, 101), (103, 7), (113, 17), (116, 20),
-    (118, 119), (122, 121), (123, 27), (64, 0), (65, 1), (67, 3), (78, 14), (80, 82), (95, 31), (110, 108), (8, 40),
-    (22, 23), (26, 122), (28, 29), (30, 29), (32, 0), (35, 3), (37, 38), (39, 40), (42, 74), (43, 11), (44, 12),
-    (46, 14), (48, 16), (50, 49), (52, 51), (53, 54), (62, 94), (63, 31), (66, 34), (68, 36), (69, 101), (70, 102),
-    (71, 72), (76, 75), (77, 45), (79, 47), (81, 82), (83, 51), (84, 116), (85, 86), (87, 86), (88, 56), (89, 121),
-    (90, 58), (91, 123), (96, 0), (97, 1), (98, 2), (99, 3), (100, 4), (104, 103), (105, 9), (107, 108), (109, 13),
-    (111, 15), (112, 113), (115, 114), (117, 118), (120, 24), (124, 92), (125, 29),
+    (2, 0), (25, 0), (3, 2), (9, 2), (4, 3), (18, 25), (121, 25), (5, 4), (24, 25), (11, 9), (32, 0), (122, 121),
+    (6, 5), (10, 9), (23, 24), (100, 4), (120, 24), (13, 11), (16, 18), (62, 32), (123, 122), (7, 6), (19, 18),
+    (42, 10), (55, 23), (101, 100), (119, 120), (124, 123), (38, 6), (39, 7), (43, 42), (48, 16), (51, 19), (54, 55),
+    (61, 62), (63, 32), (96, 0), (102, 101), (107, 11), (109, 13), (112, 16), (118, 119), (92, 124), (1, 2), (8, 9),
+    (14, 13), (15, 16), (17, 16), (22, 23), (26, 122), (30, 62), (31, 63), (35, 3), (40, 39), (41, 9), (45, 13),
+    (49, 48), (52, 51), (60, 61), (70, 38), (75, 43), (80, 112), (83, 51), (86, 54), (93, 61), (97, 96), (103, 102),
+    (108, 107), (110, 109), (115, 19), (117, 118), (64, 0), (66, 2), (90, 92), (12, 13), (20, 19), (21, 22),
+    (27, 123), (28, 60), (29, 61), (33, 1), (34, 2), (36, 35), (37, 5), (44, 45), (46, 14), (47, 15), (50, 18),
+    (53, 54), (56, 24), (57, 25), (58, 26), (59, 60), (65, 97), (67, 35), (68, 100), (69, 70), (71, 103), (72, 40),
+    (73, 41), (74, 75), (76, 108), (77, 109), (78, 110), (79, 80), (81, 49), (82, 83), (84, 52), (85, 117), (87, 86),
+    (88, 120), (89, 121), (91, 92), (94, 62), (95, 63), (98, 2), (99, 3), (104, 8), (105, 9), (106, 10), (111, 15),
+    (113, 17), (114, 18), (116, 115), (125, 93), (126, 30), (127, 31),
 )
 ORDER = (
-    (0, 1), (1, 31), (0, 96), (1, 32), (0, 31), (1, 1), (0, 32), (1, 96), (0, 64), (1, 64), (0, 3), (1, 29), (0, 33),
-    (1, 127), (0, 97), (1, 63), (0, 127), (1, 33), (0, 29), (1, 3), (0, 63), (1, 97), (0, 25), (1, 7), (0, 65),
-    (1, 95), (0, 95), (1, 65), (0, 99), (1, 61), (0, 4), (1, 28), (0, 35), (1, 125), (0, 67), (1, 93), (0, 34),
-    (1, 126), (0, 5), (1, 27), (0, 126), (1, 34), (0, 61), (1, 99), (0, 30), (1, 2), (0, 125), (1, 35), (0, 28),
-    (1, 4), (0, 24), (1, 8), (0, 121), (1, 39), (0, 57), (1, 103), (0, 9), (1, 23), (0, 36), (1, 124), (0, 100),
-    (1, 60), (0, 2), (1, 30), (0, 6), (1, 26), (0, 66), (1, 94), (0, 101), (1, 59), (0, 60), (1, 100), (0, 94),
-    (1, 66), (0, 93), (1, 67), (0, 23), (1, 9), (0, 56), (1, 104), (0, 122), (1, 38), (0, 120), (1, 40), (0, 58),
-    (1, 102), (0, 89), (1, 71), (0, 10), (1, 22), (0, 41), (1, 119), (0, 105), (1, 55), (0, 18), (1, 14), (0, 68),
-    (1, 92), (0, 98), (1, 62), (0, 7), (1, 25), (0, 38), (1, 122), (0, 102), (1, 58), (0, 69), (1, 91), (0, 12),
-    (1, 20), (0, 59), (1, 101), (0, 62), (1, 98), (0, 92), (1, 68), (0, 55), (1, 105), (0, 119), (1, 41), (0, 22),
-    (1, 10), (0, 88), (1, 72), (0, 26), (1, 6), (0, 11), (1, 21), (0, 21), (1, 11), (0, 90), (1, 70), (0, 40),
-    (1, 120), (0, 106), (1, 54), (0, 17), (1, 15), (0, 73), (1, 87), (0, 19), (1, 13), (0, 114), (1, 46), (0, 37),
-    (1, 123), (0, 103), (1, 57), (0, 70), (1, 90), (0, 13), (1, 19), (0, 108), (1, 52), (0, 44), (1, 116), (0, 54),
-    (1, 106), (0, 27), (1, 5), (0, 124), (1, 36), (0, 118), (1, 42), (0, 43), (1, 117), (0, 20), (1, 12), (0, 15),
-    (1, 17), (0, 8), (1, 24), (0, 39), (1, 121), (0, 74), (1, 86), (0, 16), (1, 16), (0, 113), (1, 47), (0, 72),
-    (1, 88), (0, 49), (1, 111), (0, 115), (1, 45), (0, 51), (1, 109), (0, 104), (1, 56), (0, 82), (1, 78), (0, 14),
-    (1, 18), (0, 45), (1, 115), (0, 109), (1, 51), (0, 107), (1, 53), (0, 86), (1, 74), (0, 123), (1, 37), (0, 53),
-    (1, 107), (0, 110), (1, 50), (0, 116), (1, 44), (0, 117), (1, 43), (0, 47), (1, 113), (0, 75), (1, 85), (0, 111),
-    (1, 49), (0, 112), (1, 48), (0, 42), (1, 118), (0, 71), (1, 89), (0, 48), (1, 112), (0, 50), (1, 110), (0, 83),
-    (1, 77), (0, 52), (1, 108), (0, 46), (1, 114), (0, 81), (1, 79), (0, 77), (1, 83), (0, 87), (1, 73), (0, 80),
-    (1, 80), (0, 91), (1, 69), (0, 78), (1, 82), (0, 85), (1, 75), (0, 84), (1, 76), (0, 79), (1, 81), (0, 76),
-    (1, 84),
+    (0, 32), (1, 96), (0, 96), (1, 32), (0, 2), (1, 30), (0, 64), (1, 64), (0, 63), (1, 97), (0, 97), (1, 63),
+    (0, 62), (1, 98), (0, 3), (1, 29), (0, 98), (1, 62), (0, 34), (1, 126), (0, 25), (1, 7), (0, 1), (1, 31), (0, 66),
+    (1, 94), (0, 31), (1, 1), (0, 95), (1, 65), (0, 65), (1, 95), (0, 61), (1, 99), (0, 30), (1, 2), (0, 4), (1, 28),
+    (0, 94), (1, 66), (0, 35), (1, 125), (0, 24), (1, 8), (0, 99), (1, 61), (0, 121), (1, 39), (0, 57), (1, 103),
+    (0, 9), (1, 23), (0, 33), (1, 127), (0, 127), (1, 33), (0, 93), (1, 67), (0, 60), (1, 100), (0, 29), (1, 3),
+    (0, 5), (1, 27), (0, 126), (1, 34), (0, 36), (1, 124), (0, 100), (1, 60), (0, 23), (1, 9), (0, 67), (1, 93),
+    (0, 122), (1, 38), (0, 120), (1, 40), (0, 56), (1, 104), (0, 18), (1, 14), (0, 10), (1, 22), (0, 89), (1, 71),
+    (0, 8), (1, 24), (0, 41), (1, 119), (0, 105), (1, 55), (0, 11), (1, 21), (0, 59), (1, 101), (0, 125), (1, 35),
+    (0, 6), (1, 26), (0, 28), (1, 4), (0, 37), (1, 123), (0, 101), (1, 59), (0, 68), (1, 92), (0, 22), (1, 10),
+    (0, 55), (1, 105), (0, 123), (1, 37), (0, 26), (1, 6), (0, 119), (1, 41), (0, 88), (1, 72), (0, 114), (1, 46),
+    (0, 19), (1, 13), (0, 42), (1, 118), (0, 50), (1, 110), (0, 16), (1, 16), (0, 106), (1, 54), (0, 104), (1, 56),
+    (0, 7), (1, 25), (0, 13), (1, 19), (0, 73), (1, 87), (0, 102), (1, 58), (0, 107), (1, 53), (0, 21), (1, 11),
+    (0, 38), (1, 122), (0, 54), (1, 106), (0, 27), (1, 5), (0, 124), (1, 36), (0, 58), (1, 102), (0, 118), (1, 42),
+    (0, 51), (1, 109), (0, 20), (1, 12), (0, 115), (1, 45), (0, 43), (1, 117), (0, 112), (1, 48), (0, 15), (1, 17),
+    (0, 48), (1, 112), (0, 17), (1, 15), (0, 39), (1, 121), (0, 14), (1, 18), (0, 109), (1, 51), (0, 12), (1, 20),
+    (0, 45), (1, 115), (0, 103), (1, 57), (0, 70), (1, 90), (0, 108), (1, 52), (0, 86), (1, 74), (0, 53), (1, 107),
+    (0, 92), (1, 68), (0, 117), (1, 43), (0, 83), (1, 77), (0, 52), (1, 108), (0, 75), (1, 85), (0, 116), (1, 44),
+    (0, 80), (1, 80), (0, 49), (1, 111), (0, 111), (1, 49), (0, 40), (1, 120), (0, 47), (1, 113), (0, 110), (1, 50),
+    (0, 113), (1, 47), (0, 44), (1, 116), (0, 46), (1, 114), (0, 69), (1, 91), (0, 77), (1, 83), (0, 87), (1, 73),
+    (0, 71), (1, 89), (0, 76), (1, 84), (0, 91), (1, 69), (0, 85), (1, 75), (0, 84), (1, 76), (0, 82), (1, 78),
+    (0, 90), (1, 70), (0, 81), (1, 79), (0, 74), (1, 86), (0, 72), (1, 88), (0, 79), (1, 81), (0, 78), (1, 82),
 )
 COLUMNS = (0, 1, 3, 2)
 
@@ -75,7 +74,7 @@
     pair, me = lax.axis_index("pair"), lax.axis_index("red")
     y, z = lax.div(pair, NZ), lax.rem(pair, NZ)
     children = plan()
-    inner = [node for node in ((0, 0), (1, 0)) + ORDER if node in children]
+    inner = [node for node in ORDER if node in children]
     sem_of = {node: NY + i for i, node in enumerate(inner)}
     pairs, slabs, occ, width = raw.shape
     group = 2 * width
@@ -157,7 +156,7 @@
     def met_copy(g):
         return pltpu.make_async_remote_copy(
             src_ref=part.at[g, 1 - core], dst_ref=met.at[g],
-            send_sem=met_send.at[g], recv_sem=met_recv.at[g],
+            send_sem=met_send, recv_sem=met_recv.at[g],
             device_id=(pair, me + 1 - 2 * core), device_id_type=MESH,
         )
 
@@ -165,8 +164,14 @@
         to = lax.rem(at_x + d, chips)
         return pltpu.make_async_remote_copy(
             src_ref=pooled.at[g, to], dst_ref=landed.at[g, at_x],
-            send_sem=red_send.at[g, d], recv_sem=red_recv.at[g, d],
+            send_sem=red_send, recv_sem=red_recv.at[g],
             device_id=(pair, to * 2 + core), device_id_type=MESH,
+        )
+
+    def all_of(ref, send, recv):
+        return pltpu.make_async_remote_copy(
+            src_ref=ref, dst_ref=ref, send_sem=send, recv_sem=recv,
+            device_id=partners[0], device_id_type=MESH,
         )
 
     def multiply(g):
@@ -189,39 +194,44 @@
     def finish(g):
         column, _ = at(-g, 0)
         value = part[g, core, at_x].astype(jnp.float32) + met[g, at_x].astype(jnp.float32)
+        all_of(landed.at[g, pl.ds(0, chips - 1)], red_send, red_recv.at[g]).wait_recv()
         for d in range(1, chips):
-            red_copy(g, d).wait_recv()
             value = value + landed[g, lax.rem(at_x + chips - d, chips)].astype(jnp.float32)
         spot = pl.ds(pl.multiple_of(column * group, group), group)
         out_ref[:, :, spot] = value.reshape(pairs, low, group).astype(jnp.bfloat16)
 
-    for half, code in inner:
-        if code:
-            copy(half, code, code).wait_recv()
-            forward(half, code)
-    before = None
-    for g in COLUMNS:
+    def await_column(g):
         outer = sum(code // NZ == g and (half, code) not in sem_of for half, code in ORDER)
         if outer:
             whole(outer, g).wait_recv()
-        multiply(g)
-        if before is not None:
-            pass_on(before)
-        before = g
-    finish(COLUMNS[0])
-    pass_on(before)
-    for g in COLUMNS[1:]:
+
+    for half, code in inner:
+        copy(half, code, code).wait_recv()
+        forward(half, code)
+    first, second, third, last = COLUMNS
+    await_column(first)
+    multiply(first)
+    await_column(second)
+    multiply(second)
+    pass_on(first)
+    await_column(third)
+    multiply(third)
+    pass_on(second)
+    pass_on(third)
+    await_column(last)
+    multiply(last)
+    finish(first)
+    pass_on(last)
+    for g in (second, third, last):
         finish(g)
 
     whole(2 * len(EDGES), 0).wait_send()
-    for g in range(NY):
-        met_copy(g).wait_send()
-        for d in range(1, chips):
-            red_copy(g, d).wait_send()
+    all_of(met, met_send, met_recv.at[0]).wait_send()
+    all_of(landed.at[:, pl.ds(0, chips - 1)], red_send, red_recv.at[0]).wait_send()
 
 
 def inner_count():
-    return len({parent for _, parent in EDGES})
+    return len({parent for _, parent in EDGES if parent})
 
 
 def local(red, amplitudes, integrals, amp_mask, kept_slab_indicator):
@@ -252,7 +262,7 @@
             pltpu.VMEM((NY, red // 2, rows // red, group), jnp.bfloat16),
             pltpu.VMEM((NY, red // 2, rows // red, group), jnp.bfloat16),
             dma((4,)), dma, dma((NY + 2 * inner_count(),)),
-            dma((NY,)), dma((NY,)), dma((NY, red // 2)), dma((NY, red // 2)),
+            dma, dma((NY,)), dma, dma((NY,)),
         ],
         compiler_params=pltpu.CompilerParams(
             collective_id=0, has_side_effects=True, vmem_limit_bytes=63 * 1024 * 1024

time: 73.1 us -> 70.4 us (0.963)
  Pallas kernels: 70.7 us -> 68 us
    pallas_call x1, Pallas kernels: 70.7 us -> 68 us  [local(): pl.pallas_call(functools.partial(kernel, red), out_shape=out, in_specs=[p...]
where the time goes in v3:
time: 70.4 us; the launch traced here: 70.3 us
  Pallas kernels  68 us (97%)
  local copies, waits for them, and re-layouts  1.57 us (2%)
    pallas_call x1, Pallas kernels, local(): pl.pallas_call(functools.partial(kernel, red), out_shape=out, in_specs=[p...  68 us
    unnamed x1, local copies, waits for them, and re-layouts  1.57 us

profile of v3, /device:TPU:1, one launch (start us, length us, event | category | flops | bytes accessed | tf_op | source)
XLA Modules:
  0.0 70.3 jit_solution(15764596328793065095)
XLA Ops:
  0.7 68.0 %shard_map.46 = bf16[8,8,1024]{2,1,0:T(8,128)(2,1)} custom-call(bf16[8,1,16,64,128]{4,3,2,1,0:T(8,128)(2,1)} %amp_ref.1, bf16[1,1,128,128]{3,2,1,0:T(8,128)(2,1)} %int_ref.1, s32[8,1,16]{2,1,0:T(1,128)} %mask_ref.1, s32[1,1]{1,0:T(1,128)S(6)} %copy.6.kept_ref), custom_call_target="tpu_custom_call" | custom-call | tf_op jit(solution)/shard_map/pallas_call | solution.py:242
  68.7 1.6 %copy.7 = bf16[8,8,1024]{2,1,0:T(8,128)(2,1)} copy(bf16[8,8,1024]{2,1,0:T(8,128)(2,1)} %shard_map.46) | data formatting | bytes 262144

commit v4 on v3

--- a/solution.py
+++ b/solution.py
@@ -104,21 +104,12 @@
             device_id=chip(0, 1), device_id_type=MESH,
         )
 
-    loads = [
-        pltpu.make_async_copy(src, dst, load_sem.at[i])
-        for i, (src, dst) in enumerate(
-            ((int_ref.at[0, 0], own), (kept_ref, flag), (mask_ref, mask), (amp_ref.at[:, 0], raw))
-        )
-    ]
-    for load in loads:
-        load.start()
-
     hops = set()
     for child, parent in EDGES:
         (cy, cz), (py, pz) = split(child), split(parent)
         hop = ((cy - py) % NY, (cz - pz) % NZ)
         hops |= {hop, (-hop[0] % NY, -hop[1] % NZ)}
-    hops = sorted(hops)
+    hops = sorted(hops, key=lambda hop: (-min(hop[1], NZ - hop[1]), hop))
     barrier = pltpu.get_barrier_semaphore()
     for hop in hops:
         pl.semaphore_signal(barrier, 1, device_id=chip(*hop), device_id_type=MESH)
@@ -127,6 +118,15 @@
     for partner in partners:
         pl.semaphore_signal(barrier, 1, device_id=partner, device_id_type=MESH)
 
+    loads = [
+        pltpu.make_async_copy(src, dst, load_sem.at[i])
+        for i, (src, dst) in enumerate(
+            ((int_ref.at[0, 0], own), (kept_ref, flag), (mask_ref, mask), (amp_ref.at[:, 0], raw))
+        )
+    ]
+    for load in loads:
+        load.start()
+
     loads[0].wait()
     loads[1].wait()
     kept = flag[0, 0].astype(jnp.float32)
@@ -188,7 +188,7 @@
     def pass_on(g):
         met_copy(g).wait_recv()
         pooled[g] = (part[g, core].astype(jnp.float32) + met[g].astype(jnp.float32)).astype(jnp.bfloat16)
-        for d in range(1, chips):
+        for d in sorted(range(1, chips), key=lambda d: -min(d, chips - d)):
             red_copy(g, d).start()
 
     def finish(g):

time: 70.4 us -> 70.3 us (level)
  no operation moved by 1% of the time
where the time goes in v4:
time: 70.3 us; the launch traced here: 70.1 us
  Pallas kernels  67.9 us (97%)
  local copies, waits for them, and re-layouts  1.57 us (2%)
    pallas_call x1, Pallas kernels, local(): pl.pallas_call(functools.partial(kernel, red), out_shape=out, in_specs=[p...  67.9 us
    unnamed x1, local copies, waits for them, and re-layouts  1.57 us

profile of v4, /device:TPU:1, one launch (start us, length us, event | category | flops | bytes accessed | tf_op | source)
XLA Modules:
  0.0 70.1 jit_solution(11205900706713331310)
XLA Ops:
  0.7 67.9 %shard_map.46 = bf16[8,8,1024]{2,1,0:T(8,128)(2,1)} custom-call(bf16[8,1,16,64,128]{4,3,2,1,0:T(8,128)(2,1)} %amp_ref.1, bf16[1,1,128,128]{3,2,1,0:T(8,128)(2,1)} %int_ref.1, s32[8,1,16]{2,1,0:T(1,128)} %mask_ref.1, s32[1,1]{1,0:T(1,128)S(6)} %copy.6.kept_ref), custom_call_target="tpu_custom_call" | custom-call | tf_op jit(solution)/shard_map/pallas_call | solution.py:242
  68.6 1.6 %copy.7 = bf16[8,8,1024]{2,1,0:T(8,128)(2,1)} copy(bf16[8,8,1024]{2,1,0:T(8,128)(2,1)} %shard_map.46) | data formatting | bytes 262144
